TPU v7x, 32 devices: a whole 2x2x4 slice. The times are simulated.
32 devices in a mesh: groups: 2 (over x), rows: 16 (over z, y, core).
Axes of the slice: x: 2, y: 2, z: 4, core: 2. Of those that a mesh axis runs over, the one named last changes fastest.
Arguments:
- depth: float32 [256, 1024], P(('groups', 'rows')), parts along dimension 0, may hold values from 0.02 to 3
- flux_x: float32 [256, 1024], P(('groups', 'rows')), parts along dimension 0, may hold values from -4 to 4
- flux_y: float32 [256, 1024], P(('groups', 'rows')), parts along dimension 0, may hold values from -4 to 4
- elevation: float32 [256, 1024], P(('groups', 'rows')), parts along dimension 0, may hold values from -6 to 6
- roughness: float32 [256, 1024], P(('groups', 'rows')), parts along dimension 0, may hold values from 0.02 to 0.1
- wet_tiles: int32 [32, 128], P(('groups', 'rows')), parts along dimension 0, may hold values 0 or 1
- chan_depth: float32 [1536, 128], P(('groups', 'rows')), parts along dimension 0, may hold values from 0.5 to 5
- chan_flow: float32 [1536, 128], P(('groups', 'rows')), parts along dimension 0, may hold values from -8 to 8
- chan_bed: float32 [1536, 128], P(('groups', 'rows')), parts along dimension 0, may hold values from -6 to 6
- chan_width: float32 [1536, 128], P(('groups', 'rows')), parts along dimension 0, may hold values from 20 to 200
- lateral_owner: int32 [1536, 1], P(('groups', 'rows')), parts along dimension 0, may hold values from 0 to 15; in each aligned block of 48 rows (0 to 47, 48 to 95, ...) at most 9 rows name the same one
- lateral_row: int32 [1536], P(('groups', 'rows')), parts along dimension 0, may hold values from 0 to 7
- reach_offset: int32 [1536], P(('groups', 'rows')), parts along dimension 0, may hold values from 0 to 896
Outputs:
- depth_out: float32 [256, 1024], P(('groups', 'rows')), parts along dimension 0
- flux_x_out: float32 [256, 1024], P(('groups', 'rows')), parts along dimension 0
- flux_y_out: float32 [256, 1024], P(('groups', 'rows')), parts along dimension 0
- chan_depth_out: float32 [1536, 128], P(('groups', 'rows')), parts along dimension 0
- chan_flow_out: float32 [1536, 128], P(('groups', 'rows')), parts along dimension 0
There are 2 independent parts, one for each index of `groups`. A program takes and returns all parts, laid end to end along the dimension named above; each array names one. Nothing has to cross between parts.
Inputs may be any that keep to these rules, and one draw needn't show every extreme that they name: `lateral_owner`: among the 48 reaches of one device (aligned blocks), no device index is named more than 9 times.
All inputs are finite; a program needn't handle non-finite values. No bound on the sum of `wet_tiles` on one device may be relied on, other than what follows from the above.
Results may differ from a plain program's by a relative error of at most 0.00002.
Values sent between devices are 32-bit elements; how exact they have to be, the bound alone decides.
A program may use at most 64 MiB of HBM per device.

v0:
```python
import functools

import jax
import jax.numpy as jnp
from jax import lax
from jax.experimental import pallas as pl
from jax.experimental.pallas import tpu as pltpu
from jax.sharding import PartitionSpec as P

TILE = 8
LANES = 128

GRAVITY = 9.81
TIME_STEP = 5.0
CELL_SIZE = 90.0
DEPTH_FLOOR = 0.05
EXCHANGE_COEF = 40.0
CHANNEL_MANNING = 0.035

F32 = jnp.float32
BF16 = jnp.bfloat16
MESH = pl.DeviceIdType.MESH


def face_flux(flux, upper_a, upper_b, floor_a, floor_b, manning, active):
    flow_depth = jnp.maximum(jnp.maximum(upper_a, upper_b) - jnp.maximum(floor_a, floor_b), 0.0)
    slope = (upper_b - upper_a) * (GRAVITY * TIME_STEP / CELL_SIZE)
    inverse = jnp.exp((-7.0 / 3.0) * jnp.log(jnp.maximum(flow_depth, DEPTH_FLOOR)))
    return (
        active
        * (flux - flow_depth * slope)
        / (1.0 + (GRAVITY * TIME_STEP) * manning * manning * jnp.abs(flux) * inverse)
    )


def iota(shape, axis):
    return lax.broadcasted_iota(jnp.int32, shape, axis)


def split3(x):
    high = x.astype(BF16)
    rest = x - high.astype(F32)
    mid = rest.astype(BF16)
    low = (rest - mid.astype(F32)).astype(BF16)
    return jnp.concatenate([high, mid, low], axis=1)


def join3(x):
    width = x.shape[1] // 3
    return (x[:, 2 * width :] + x[:, width : 2 * width]) + x[:, :width]


def pick(onehot, x):
    return join3(jnp.dot(onehot, split3(x), preferred_element_type=F32))


def pick_t(onehot, x):
    return join3(
        lax.dot_general(
            onehot, split3(x), (((0,), (0,)), ((), ())), preferred_element_type=F32
        )
    )


def roll_rows(x, amount, to_right):
    for bit in range(7):
        step = 1 << bit
        turned = pltpu.roll(x, step if to_right else LANES - step, 1)
        x = jnp.where((amount & step) != 0, turned, x)
    return x


def kernel(n, cap, cpad, *refs):
    (
        depth_h, fx_h, fy_h, el_h, ro_h, wet_h, cd_h, cf_h, cb_h, cw_h, own_h, row_h, off_h,
        depth_w, fx_w, fy_w, cd_w, cf_w,
        depth_v, fx_v, fy_v, el_v, ro_v, wet_v, cd_v, cf_v, cb_v, cw_v, own_v, row_v, off_v,
        send_a, recv_a, send_b, recv_b, back_a, home_a, back_b, home_b,
        up_s, down_s, below_r, above_r, up2_s, down2_s, below2_r, above2_r,
        in_sem, sa, ra, sb, rb, sc, rc, sd, rd, hs, hr,
    ) = refs
    me = lax.axis_index("rows")
    rows, columns = depth_v.shape
    blocks = columns // LANES
    cells = rows * blocks
    reaches, nodes = cd_v.shape
    slots = n * cpad

    inputs = [
        pltpu.make_async_copy(h, v, in_sem.at[i])
        for i, (h, v) in enumerate(
            [
                (own_h, own_v), (row_h, row_v), (off_h, off_v), (cb_h, cb_v), (cd_h, cd_v),
                (depth_h, depth_v), (el_h, el_v), (ro_h, ro_v), (fy_h, fy_v), (wet_h, wet_v),
                (cf_h, cf_v), (cw_h, cw_v), (fx_h, fx_v),
            ]
        )
    ]
    for copy in inputs:
        copy.start()

    for ref in (recv_a, recv_b, home_a, home_b):
        ref[...] = jnp.zeros_like(ref)

    barrier = pltpu.get_barrier_semaphore()

    def greet(k, _):
        pl.semaphore_signal(
            barrier, inc=1, device_id={"rows": lax.rem(me + k, n)}, device_id_type=MESH
        )
        return _

    lax.fori_loop(1, n, greet, 0)

    for copy in inputs[:5]:
        copy.wait()
    owner_r = own_v[...]
    offset_r = off_v[...]
    key_r = (offset_r >> 7) * rows + row_v[...]
    turn_r = offset_r & (LANES - 1)
    ri, ci = iota((reaches, reaches), 0), iota((reaches, reaches), 1)

    def column(v):
        wide = jnp.broadcast_to(v.astype(F32), (reaches, reaches))
        return jnp.sum(jnp.where(ri == ci, wide, 0.0), axis=1, keepdims=True)

    owner_f = owner_r.astype(F32)
    owner_c, key_c, turn_c = column(owner_r), column(key_r), column(turn_r)
    same = jnp.where(owner_c == owner_f, 1.0, 0.0)
    rank_c = jnp.sum(jnp.where(ci < ri, same, 0.0), axis=1, keepdims=True)
    rank_r = jnp.sum(jnp.where(ri < ci, same, 0.0), axis=0, keepdims=True)
    slot_r = (owner_f * cpad + rank_r).astype(jnp.int32)
    slot_c = (owner_c * cpad + rank_c).astype(jnp.int32)
    pack = jnp.where(iota((slots, reaches), 0) == slot_r, 1.0, 0.0).astype(BF16)
    unpack = jnp.where(iota((reaches, slots), 1) == slot_c, 1.0, 0.0).astype(BF16)

    bed = cb_v[...]
    cdepth = cd_v[...]
    csurf = bed + cdepth
    send_a[...] = pick(pack, csurf).reshape(n, cpad, nodes)
    lane = iota((reaches, LANES), 1)
    rank_i = rank_c.astype(jnp.int32)
    ids = jnp.where(
        lane == rank_i, key_c + 1.0, jnp.where(lane == rank_i + 64, turn_c, 0.0)
    ).astype(BF16)
    to_owner = jnp.where(iota((n, reaches), 0) == owner_r, 1.0, 0.0).astype(BF16)
    id_rows = jnp.dot(to_owner, ids, preferred_element_type=F32)
    for d in range(n):
        send_a[d, cap : cap + 1, :] = id_rows[d : d + 1, :]

    for copy in inputs[5:10]:
        copy.wait()
    depth, el, ro = depth_v[...], el_v[...], ro_v[...]
    fy = fy_v[...]
    tiles = wet_v[...].astype(F32)
    last = rows - 1
    up_s[0:1, :] = depth[0:1]
    up_s[1:2, :] = el[0:1]
    up_s[2:3, :] = ro[0:1]
    up_s[3:4, :] = fy[0:1]
    up_s[4:5, :] = jnp.zeros((1, columns), F32)
    up_s[4:5, 0 : tiles.shape[1]] = tiles
    down_s[0:1, :] = depth[last:]
    down_s[1:2, :] = el[last:]
    down_s[2:3, :] = ro[last:]
    down_s[3:4, :] = fy[last:]
    down_s[4:5, :] = jnp.zeros((1, columns), F32)
    down_s[4:5, 0 : tiles.shape[1]] = tiles

    def exchange(source, target, span, send_sem, recv_sem):
        def make(k):
            peer = lax.rem(me + k, n)
            return pltpu.make_async_remote_copy(
                src_ref=source.at[(peer,) + span],
                dst_ref=target.at[(me,) + span],
                send_sem=send_sem.at[k],
                recv_sem=recv_sem.at[k],
                device_id={"rows": peer},
                device_id_type=MESH,
            )

        def start():
            def one(k, _):
                make(k).start()
                return _

            lax.fori_loop(1, n, one, 0)
            target[me] = source[me]

        def arrive():
            def one(k, _):
                make(k).wait_recv()
                return _

            lax.fori_loop(1, n, one, 0)

        def leave():
            def one(k, _):
                make(k).wait_send()
                return _

            lax.fori_loop(1, n, one, 0)

        return start, arrive, leave

    a_span = (pl.ds(0, cap + 1),)
    b_span = (slice(None), pl.ds(0, cap))
    v_span = (pl.ds(0, cap),)
    start_a, arrive_a, leave_a = exchange(send_a, recv_a, a_span, sa, ra)
    start_b, arrive_b, leave_b = exchange(send_b, recv_b, b_span, sb, rb)
    start_c, arrive_c, leave_c = exchange(back_a, home_a, v_span, sc, rc)
    start_d, arrive_d, leave_d = exchange(back_b, home_b, v_span, sd, rd)

    above, below = lax.rem(me + n - 1, n), lax.rem(me + 1, n)

    def halo(src, dst, i, peer):
        return pltpu.make_async_remote_copy(
            src_ref=src, dst_ref=dst, send_sem=hs.at[i], recv_sem=hr.at[i],
            device_id={"rows": peer}, device_id_type=MESH,
        )

    halos = [halo(up_s, below_r, 0, above), halo(down_s, above_r, 1, below)]
    halos2 = [halo(up2_s, below2_r, 2, above), halo(down2_s, above2_r, 3, below)]

    pl.semaphore_wait(barrier, n - 1)
    start_a()
    for copy in halos:
        copy.start()

    for copy in inputs[10:]:
        copy.wait()
    node = iota((reaches, nodes), 1)
    inner = jnp.where(node < nodes - 1, 1.0, 0.0)
    bed_next = pltpu.roll(bed, nodes - 1, 1)

    def channel_flow(flow, surface):
        return face_flux(
            flow, surface, pltpu.roll(surface, nodes - 1, 1), bed, bed_next,
            CHANNEL_MANNING, inner,
        )

    def channel_inflow(flow):
        return (TIME_STEP / CELL_SIZE) * (pltpu.roll(flow, 1, 1) - flow)

    cflow = channel_flow(cf_v[...], csurf)
    cpart = cdepth + channel_inflow(cflow)
    per_width = TIME_STEP / (cw_v[...] * CELL_SIZE)
    send_b[:, 0] = pick(pack, bed).reshape(n, cpad, nodes)
    send_b[:, 1] = pick(pack, cpart).reshape(n, cpad, nodes)
    send_b[:, 2] = pick(pack, per_width).reshape(n, cpad, nodes)
    start_b()

    col = iota((rows, columns), 1)
    row = iota((rows, columns), 0)
    spread = jnp.where(
        iota((tiles.shape[1], columns), 0) == iota((tiles.shape[1], columns), 1) // TILE, 1.0, 0.0
    ).astype(BF16)

    def expand(t):
        wide = jnp.broadcast_to(t, (rows, t.shape[1])).astype(BF16)
        return jnp.dot(wide, spread, preferred_element_type=F32)

    wet = expand(tiles)
    el_right = pltpu.roll(el, columns - 1, 1)
    man_x = 0.5 * (ro + pltpu.roll(ro, columns - 1, 1))
    act_x = jnp.where(
        col < columns - 1, jnp.maximum(wet, pltpu.roll(wet, columns - 1, 1)), 0.0
    )

    def flood_x(flux, surface):
        return face_flux(
            flux, surface, pltpu.roll(surface, columns - 1, 1), el, el_right, man_x, act_x
        )

    def to_cells(x):
        return jnp.concatenate([x[:, b * LANES : (b + 1) * LANES] for b in range(blocks)], axis=0)

    def to_grid(x):
        return jnp.concatenate([x[b * rows : (b + 1) * rows] for b in range(blocks)], axis=1)

    surface = el + depth
    fx = flood_x(fx_v[...], surface)

    for copy in halos:
        copy.wait_recv()

    def shift_up(x, edge):
        return jnp.where(row == last, edge, pltpu.roll(x, rows - 1, 0))

    def shift_down(x, edge):
        return jnp.where(row == 0, edge, pltpu.roll(x, 1, 0))

    edge_below = jnp.where(me == n - 1, 0.0, 1.0)
    edge_above = jnp.where(me == 0, 0.0, 1.0)
    wet_below = expand(below_r[4:5, 0 : tiles.shape[1]])
    wet_above = expand(above_r[4:5, 0 : tiles.shape[1]])[0:1]
    el_below = below_r[1:2, :]
    el_down = shift_up(el, el_below)
    man_y = 0.5 * (ro + shift_up(ro, below_r[2:3, :]))
    act_y = jnp.where(row == last, edge_below, 1.0) * jnp.maximum(wet, wet_below * 1.0)
    act_y = jnp.where(row == last, act_y, wet)
    el_above = above_r[1:2, :]
    man_top = 0.5 * (above_r[2:3, :] + ro[0:1])
    act_top = edge_above * jnp.maximum(wet_above, wet[0:1])

    def flood_y(flux, top, surface, below_row, above_row):
        new = face_flux(
            flux, surface, shift_up(surface, below_row), el, el_down, man_y, act_y
        )
        new_top = face_flux(top, above_row, surface[0:1], el_above, el[0:1], man_top, act_top)
        return new, new_top

    fy, top = flood_y(
        fy, above_r[3:4, :], surface, el_below + below_r[0:1, :], el_above + above_r[0:1, :]
    )

    def inflow(fx, fy, top):
        return (TIME_STEP / CELL_SIZE) * (
            pltpu.roll(fx, 1, 1) - fx + shift_down(fy, top) - fy
        )

    part = depth + inflow(fx, fy, top)

    arrive_a()
    packed = recv_a[...]
    wide_ids = jnp.broadcast_to(packed[:, cap : cap + 1, :], (n, cpad, LANES))
    mine = (iota((n, cpad, LANES), 2) & 63) == iota((n, cpad, LANES), 1)
    kept = jnp.where(mine, wide_ids, 0.0).reshape(slots, LANES).astype(BF16)
    halves = jnp.where(
        (iota((LANES, 2 * LANES), 0) < 64) == (iota((LANES, 2 * LANES), 1) < LANES), 1.0, 0.0
    ).astype(BF16)
    decoded = jnp.dot(kept, halves, preferred_element_type=F32).astype(jnp.int32)
    key = decoded[:, :LANES] - 1
    turn = decoded[:, LANES:]
    cell = iota((slots, cells), 1)
    key_cells = key[:, :cells]
    first = jnp.where(cell == key_cells, 1.0, 0.0).astype(BF16)
    second = jnp.where(
        (cell == key_cells + rows) & (key_cells >= 0), 1.0, 0.0
    ).astype(BF16)
    both = jnp.concatenate([first, second], axis=0)
    right = iota((slots, LANES), 1) >= turn

    def windows(surface):
        found = pick(both, to_cells(surface))
        return roll_rows(jnp.where(right, found[:slots], found[slots:]), turn, False)

    def gains(lateral):
        turned = roll_rows(lateral, turn, True)
        halves = jnp.concatenate(
            [jnp.where(right, turned, 0.0), jnp.where(right, 0.0, turned)], axis=0
        )
        return (TIME_STEP / (CELL_SIZE * CELL_SIZE)) * to_grid(pick_t(both, halves))

    csurf_s = packed.reshape(slots, nodes)
    lateral = EXCHANGE_COEF * (csurf_s - windows(surface))
    back_a[...] = lateral.reshape(n, cpad, nodes)
    start_c()
    depth = jnp.maximum(part + gains(lateral), 0.0)
    up2_s[...] = depth[0:1]
    down2_s[...] = depth[last:]
    for copy in halos2:
        copy.start()

    surface = el + depth
    found = windows(surface)
    arrive_b()
    bed_s = recv_b[:, 0].reshape(slots, nodes)
    cpart_s = recv_b[:, 1].reshape(slots, nodes)
    width_s = recv_b[:, 2].reshape(slots, nodes)
    lateral2 = EXCHANGE_COEF * (bed_s + jnp.maximum(cpart_s - lateral * width_s, 0.0) - found)
    back_b[...] = lateral2.reshape(n, cpad, nodes)
    start_d()
    gained = gains(lateral2)

    fx = flood_x(fx, surface)
    fx_w[...] = fx
    for copy in halos2:
        copy.wait_recv()
    fy, top = flood_y(fy, top, surface, el_below + below2_r[...], el_above + above2_r[...])
    fy_w[...] = fy
    depth_w[...] = jnp.maximum(depth + inflow(fx, fy, top) + gained, 0.0)

    arrive_c()
    cdepth = jnp.maximum(
        cpart - per_width * pick(unpack, home_a[...].reshape(slots, nodes)), 0.0
    )
    cflow = channel_flow(cflow, bed + cdepth)
    cf_w[...] = cflow
    cpart = cdepth + channel_inflow(cflow)
    arrive_d()
    cd_w[...] = jnp.maximum(
        cpart - per_width * pick(unpack, home_b[...].reshape(slots, nodes)), 0.0
    )

    leave_a()
    leave_b()
    leave_c()
    leave_d()
    for copy in halos + halos2:
        copy.wait_send()


def write_out(*refs):
    copies = [pltpu.make_async_copy(refs[i], refs[5 + i], refs[10].at[i]) for i in range(5)]
    for copy in copies:
        copy.start()
    for copy in copies:
        copy.wait()


def per_device(
    depth, flux_x, flux_y, elevation, roughness, wet_tiles, chan_depth, chan_flow, chan_bed,
    chan_width, lateral_owner, lateral_row, reach_offset,
):
    n = lax.axis_size("rows")
    rows, columns = depth.shape
    reaches, nodes = chan_depth.shape
    cap = max(2, (3 * reaches + n - 1) // n)
    cpad = -(-(cap + 1) // 8) * 8
    operands = (
        depth, flux_x, flux_y, elevation, roughness, wet_tiles, chan_depth, chan_flow,
        chan_bed, chan_width, lateral_owner.reshape(1, reaches),
        lateral_row.reshape(1, reaches), reach_offset.reshape(1, reaches),
    )
    grid_like = jax.ShapeDtypeStruct((rows, columns), F32)
    chan_like = jax.ShapeDtypeStruct((reaches, nodes), F32)
    block = pltpu.VMEM((n, cpad, nodes), F32)
    triple = pltpu.VMEM((n, 3, cpad, nodes), F32)
    halo = pltpu.VMEM((5, columns), F32)
    line = pltpu.VMEM((1, columns), F32)
    dma = pltpu.SemaphoreType.DMA
    shapes = (grid_like, grid_like, grid_like, chan_like, chan_like)
    results = pl.pallas_call(
        functools.partial(kernel, n, cap, cpad),
        out_shape=shapes,
        in_specs=[pl.BlockSpec(memory_space=pltpu.HBM)] * len(operands),
        out_specs=[pl.BlockSpec(memory_space=pltpu.VMEM)] * 5,
        scratch_shapes=[pltpu.VMEM(x.shape, x.dtype) for x in operands]
        + [block, block, triple, triple, block, block, block, block]
        + [halo] * 4
        + [line] * 4
        + [dma((13,))]
        + [dma((n,))] * 8
        + [dma((4,)), dma((4,))],
        compiler_params=pltpu.CompilerParams(
            collective_id=0, has_side_effects=True, vmem_limit_bytes=24 * 1024 * 1024
        ),
    )(*[pltpu.with_memory_space_constraint(x, pltpu.HBM) for x in operands])
    return pl.pallas_call(
        write_out,
        out_shape=shapes,
        in_specs=[pl.BlockSpec(memory_space=pl.ANY)] * 5,
        out_specs=[pl.BlockSpec(memory_space=pltpu.HBM)] * 5,
        scratch_shapes=[dma((5,))],
        compiler_params=pltpu.CompilerParams(vmem_limit_bytes=4 * 1024 * 1024),
    )(*results)


def solution(mesh):
    spec2 = P(("groups", "rows"), None)
    spec1 = P(("groups", "rows"))
    return jax.shard_map(
        per_device,
        mesh=mesh,
        in_specs=(spec2,) * 11 + (spec1,) * 2,
        out_specs=(spec2,) * 5,
        check_vma=False,
    )
```

profile of v0, /device:TPU:0, one launch (start us, length us, event | category | flops | bytes accessed | tf_op | source)
XLA Modules:
  0.0 23.7 jit_solution(12103711816240963065)
XLA Ops:
  0.6 22.4 %shard_map.164 = (f32[8,1024]{1,0:T(8,128)S(1)}, f32[8,1024]{1,0:T(8,128)S(1)}, f32[8,1024]{1,0:T(8,128)S(1)}, f32[48,128]{1,0:T(8,128)S(1)}, f32[48,128]{1,0:T(8,128)S(1)}) custom-call(f32[8,1024]{1,0:T(8,128)} %refs_0_.1, f32[8,1024]{1,0:T(8,128)} %refs_1_.1, f32[8,1024]{1,0:T(8,128)} %refs_2_.1, f32[8,1024]{1,0:T(8,128)} %refs_3_.1, f32[8,1024]{1,0:T(8,128)} %refs_4_.1, ...), custom_call_target="tpu_custom_call" | custom-call | tf_op jit(solution)/shard_map/pallas_call | solution.py:434
  23.0 0.7 %shard_map.165 = (f32[8,1024]{1,0:T(8,128)}, f32[8,1024]{1,0:T(8,128)}, f32[8,1024]{1,0:T(8,128)}, f32[48,128]{1,0:T(8,128)}, f32[48,128]{1,0:T(8,128)}) custom-call(f32[8,1024]{1,0:T(8,128)S(1)} %get-tuple-element.10.refs_0_, f32[8,1024]{1,0:T(8,128)S(1)} %get-tuple-element.11.refs_1_, f32[8,1024]{1,0:T(8,128)S(1)} %get-tuple-element.12.refs_2_, ...), custom_call_target="tpu_custom_call" | custom-call | tf_op jit(solution)/shard_map/pallas_call | solution.py:450
where the time goes:
time: 23.9 us; the launch traced here: 23.7 us
  Pallas kernels  23.1 us (97%)
  between operations  0.64 us (3%)
    pallas_call x1, Pallas kernels, per_device(): pl.pallas_call(functools.partial(kernel, n, cap, cpad), out_shape=shapes,...  22.4 us
    pallas_call x1, Pallas kernels, per_device(): pl.pallas_call(write_out, out_shape=shapes, in_specs=[pl.BlockSpec(memory...  0.7 us

commit v1 on v0

--- a/solution.py
+++ b/solution.py
@@ -63,11 +63,8 @@
 
 
 def roll_rows(x, amount, to_right):
-    for bit in range(7):
-        step = 1 << bit
-        turned = pltpu.roll(x, step if to_right else LANES - step, 1)
-        x = jnp.where((amount & step) != 0, turned, x)
-    return x
+    source = iota(x.shape, 1) + (LANES - amount if to_right else amount)
+    return jnp.take_along_axis(x, source & (LANES - 1), axis=1, mode="promise_in_bounds")
 
 
 def kernel(n, cap, cpad, *refs):
@@ -75,9 +72,9 @@
         depth_h, fx_h, fy_h, el_h, ro_h, wet_h, cd_h, cf_h, cb_h, cw_h, own_h, row_h, off_h,
         depth_w, fx_w, fy_w, cd_w, cf_w,
         depth_v, fx_v, fy_v, el_v, ro_v, wet_v, cd_v, cf_v, cb_v, cw_v, own_v, row_v, off_v,
-        send_a, recv_a, send_b, recv_b, back_a, home_a, back_b, home_b,
+        send_a, recv_a, send_b, recv_b, back_b, home_b,
         up_s, down_s, below_r, above_r, up2_s, down2_s, below2_r, above2_r,
-        in_sem, sa, ra, sb, rb, sc, rc, sd, rd, hs, hr,
+        in_sem, sa, ra, sb, rb, sd, rd, hs, hr,
     ) = refs
     me = lax.axis_index("rows")
     rows, columns = depth_v.shape
@@ -99,7 +96,7 @@
     for copy in inputs:
         copy.start()
 
-    for ref in (recv_a, recv_b, home_a, home_b):
+    for ref in (recv_a, recv_b, home_b):
         ref[...] = jnp.zeros_like(ref)
 
     barrier = pltpu.get_barrier_semaphore()
@@ -205,11 +202,9 @@
 
     a_span = (pl.ds(0, cap + 1),)
     b_span = (slice(None), pl.ds(0, cap))
-    v_span = (pl.ds(0, cap),)
     start_a, arrive_a, leave_a = exchange(send_a, recv_a, a_span, sa, ra)
     start_b, arrive_b, leave_b = exchange(send_b, recv_b, b_span, sb, rb)
-    start_c, arrive_c, leave_c = exchange(back_a, home_a, v_span, sc, rc)
-    start_d, arrive_d, leave_d = exchange(back_b, home_b, v_span, sd, rd)
+    start_d, arrive_d, leave_d = exchange(back_b, home_b, b_span, sd, rd)
 
     above, below = lax.rem(me + n - 1, n), lax.rem(me + 1, n)
 
@@ -221,11 +216,6 @@
 
     halos = [halo(up_s, below_r, 0, above), halo(down_s, above_r, 1, below)]
     halos2 = [halo(up2_s, below2_r, 2, above), halo(down2_s, above2_r, 3, below)]
-
-    pl.semaphore_wait(barrier, n - 1)
-    start_a()
-    for copy in halos:
-        copy.start()
 
     for copy in inputs[10:]:
         copy.wait()
@@ -248,6 +238,10 @@
     send_b[:, 0] = pick(pack, bed).reshape(n, cpad, nodes)
     send_b[:, 1] = pick(pack, cpart).reshape(n, cpad, nodes)
     send_b[:, 2] = pick(pack, per_width).reshape(n, cpad, nodes)
+    pl.semaphore_wait(barrier, n - 1)
+    start_a()
+    for copy in halos:
+        copy.start()
     start_b()
 
     col = iota((rows, columns), 1)
@@ -354,8 +348,7 @@
 
     csurf_s = packed.reshape(slots, nodes)
     lateral = EXCHANGE_COEF * (csurf_s - windows(surface))
-    back_a[...] = lateral.reshape(n, cpad, nodes)
-    start_c()
+    back_b[:, 0] = lateral.reshape(n, cpad, nodes)
     depth = jnp.maximum(part + gains(lateral), 0.0)
     up2_s[...] = depth[0:1]
     down2_s[...] = depth[last:]
@@ -369,7 +362,7 @@
     cpart_s = recv_b[:, 1].reshape(slots, nodes)
     width_s = recv_b[:, 2].reshape(slots, nodes)
     lateral2 = EXCHANGE_COEF * (bed_s + jnp.maximum(cpart_s - lateral * width_s, 0.0) - found)
-    back_b[...] = lateral2.reshape(n, cpad, nodes)
+    back_b[:, 1] = lateral2.reshape(n, cpad, nodes)
     start_d()
     gained = gains(lateral2)
 
@@ -381,21 +374,19 @@
     fy_w[...] = fy
     depth_w[...] = jnp.maximum(depth + inflow(fx, fy, top) + gained, 0.0)
 
-    arrive_c()
+    arrive_d()
     cdepth = jnp.maximum(
-        cpart - per_width * pick(unpack, home_a[...].reshape(slots, nodes)), 0.0
+        cpart - per_width * pick(unpack, home_b[:, 0].reshape(slots, nodes)), 0.0
     )
     cflow = channel_flow(cflow, bed + cdepth)
     cf_w[...] = cflow
     cpart = cdepth + channel_inflow(cflow)
-    arrive_d()
     cd_w[...] = jnp.maximum(
-        cpart - per_width * pick(unpack, home_b[...].reshape(slots, nodes)), 0.0
+        cpart - per_width * pick(unpack, home_b[:, 1].reshape(slots, nodes)), 0.0
     )
 
     leave_a()
     leave_b()
-    leave_c()
     leave_d()
     for copy in halos + halos2:
         copy.wait_send()
@@ -426,6 +417,7 @@
     grid_like = jax.ShapeDtypeStruct((rows, columns), F32)
     chan_like = jax.ShapeDtypeStruct((reaches, nodes), F32)
     block = pltpu.VMEM((n, cpad, nodes), F32)
+    double = pltpu.VMEM((n, 2, cpad, nodes), F32)
     triple = pltpu.VMEM((n, 3, cpad, nodes), F32)
     halo = pltpu.VMEM((5, columns), F32)
     line = pltpu.VMEM((1, columns), F32)
@@ -437,11 +429,11 @@
         in_specs=[pl.BlockSpec(memory_space=pltpu.HBM)] * len(operands),
         out_specs=[pl.BlockSpec(memory_space=pltpu.VMEM)] * 5,
         scratch_shapes=[pltpu.VMEM(x.shape, x.dtype) for x in operands]
-        + [block, block, triple, triple, block, block, block, block]
+        + [block, block, triple, triple, double, double]
         + [halo] * 4
         + [line] * 4
         + [dma((13,))]
-        + [dma((n,))] * 8
+        + [dma((n,))] * 6
         + [dma((4,)), dma((4,))],
         compiler_params=pltpu.CompilerParams(
             collective_id=0, has_side_effects=True, vmem_limit_bytes=24 * 1024 * 1024

time: 23.9 us -> 22.7 us (0.950)
  Pallas kernels: 23.1 us -> 21.9 us
    pallas_call x1, Pallas kernels: 22.4 us -> 21.2 us  [per_device(): pl.pallas_call(functools.partial(kernel, n, cap, cpad), out_shape=shapes,...]
where the time goes in v1:
time: 22.7 us; the launch traced here: 22.5 us
  Pallas kernels  21.9 us (96%)
  between operations  0.64 us (3%)
    pallas_call x1, Pallas kernels, per_device(): pl.pallas_call(functools.partial(kernel, n, cap, cpad), out_shape=shapes,...  21.2 us
    pallas_call x1, Pallas kernels, per_device(): pl.pallas_call(write_out, out_shape=shapes, in_specs=[pl.BlockSpec(memory...  0.7 us

profile of v1, /device:TPU:0, one launch (start us, length us, event | category | flops | bytes accessed | tf_op | source)
XLA Modules:
  0.0 22.5 jit_solution(9196323793991826065)
XLA Ops:
  0.6 21.2 %shard_map.164 = (f32[8,1024]{1,0:T(8,128)S(1)}, f32[8,1024]{1,0:T(8,128)S(1)}, f32[8,1024]{1,0:T(8,128)S(1)}, f32[48,128]{1,0:T(8,128)S(1)}, f32[48,128]{1,0:T(8,128)S(1)}) custom-call(f32[8,1024]{1,0:T(8,128)} %refs_0_.1, f32[8,1024]{1,0:T(8,128)} %refs_1_.1, f32[8,1024]{1,0:T(8,128)} %refs_2_.1, f32[8,1024]{1,0:T(8,128)} %refs_3_.1, f32[8,1024]{1,0:T(8,128)} %refs_4_.1, ...), custom_call_target="tpu_custom_call" | custom-call | tf_op jit(solution)/shard_map/pallas_call | solution.py:426
  21.9 0.7 %shard_map.165 = (f32[8,1024]{1,0:T(8,128)}, f32[8,1024]{1,0:T(8,128)}, f32[8,1024]{1,0:T(8,128)}, f32[48,128]{1,0:T(8,128)}, f32[48,128]{1,0:T(8,128)}) custom-call(f32[8,1024]{1,0:T(8,128)S(1)} %get-tuple-element.10.refs_0_, f32[8,1024]{1,0:T(8,128)S(1)} %get-tuple-element.11.refs_1_, f32[8,1024]{1,0:T(8,128)S(1)} %get-tuple-element.12.refs_2_, ...), custom_call_target="tpu_custom_call" | custom-call | tf_op jit(solution)/shard_map/pallas_call | solution.py:442

commit v2 on v1

--- a/solution.py
+++ b/solution.py
@@ -181,7 +181,7 @@
                 make(k).start()
                 return _
 
-            lax.fori_loop(1, n, one, 0)
+            lax.fori_loop(1, n, one, 0, unroll=3)
             target[me] = source[me]
 
         def arrive():
@@ -189,14 +189,14 @@
                 make(k).wait_recv()
                 return _
 
-            lax.fori_loop(1, n, one, 0)
+            lax.fori_loop(1, n, one, 0, unroll=3)
 
         def leave():
             def one(k, _):
                 make(k).wait_send()
                 return _
 
-            lax.fori_loop(1, n, one, 0)
+            lax.fori_loop(1, n, one, 0, unroll=3)
 
         return start, arrive, leave
 

time: 22.7 us -> 22.6 us (level)
  no operation moved by 1% of the time
where the time goes in v2:
time: 22.6 us; the launch traced here: 22.4 us
  Pallas kernels  21.7 us (96%)
  between operations  0.64 us (3%)
    pallas_call x1, Pallas kernels, per_device(): pl.pallas_call(functools.partial(kernel, n, cap, cpad), out_shape=shapes,...  21 us
    pallas_call x1, Pallas kernels, per_device(): pl.pallas_call(write_out, out_shape=shapes, in_specs=[pl.BlockSpec(memory...  0.7 us

profile of v2, /device:TPU:0, one launch (start us, length us, event | category | flops | bytes accessed | tf_op | source)
XLA Modules:
  0.0 22.4 jit_solution(1887419766094690432)
XLA Ops:
  0.6 21.0 %shard_map.164 = (f32[8,1024]{1,0:T(8,128)S(1)}, f32[8,1024]{1,0:T(8,128)S(1)}, f32[8,1024]{1,0:T(8,128)S(1)}, f32[48,128]{1,0:T(8,128)S(1)}, f32[48,128]{1,0:T(8,128)S(1)}) custom-call(f32[8,1024]{1,0:T(8,128)} %refs_0_.1, f32[8,1024]{1,0:T(8,128)} %refs_1_.1, f32[8,1024]{1,0:T(8,128)} %refs_2_.1, f32[8,1024]{1,0:T(8,128)} %refs_3_.1, f32[8,1024]{1,0:T(8,128)} %refs_4_.1, ...), custom_call_target="tpu_custom_call" | custom-call | tf_op jit(solution)/shard_map/pallas_call | solution.py:426
  21.7 0.7 %shard_map.165 = (f32[8,1024]{1,0:T(8,128)}, f32[8,1024]{1,0:T(8,128)}, f32[8,1024]{1,0:T(8,128)}, f32[48,128]{1,0:T(8,128)}, f32[48,128]{1,0:T(8,128)}) custom-call(f32[8,1024]{1,0:T(8,128)S(1)} %get-tuple-element.10.refs_0_, f32[8,1024]{1,0:T(8,128)S(1)} %get-tuple-element.11.refs_1_, f32[8,1024]{1,0:T(8,128)S(1)} %get-tuple-element.12.refs_2_, ...), custom_call_target="tpu_custom_call" | custom-call | tf_op jit(solution)/shard_map/pallas_call | solution.py:442
